TPU v7x, 256 devices: a whole 4x4x8 slice. The times are simulated.
256 devices in a mesh: blk: 64 (over z_hi, y, x, core), group: 4 (over z_lo).
Axes of the slice: x: 4, y: 4, z: 8 (z_hi: 2, z_lo: 4; z = z_hi * 4 + z_lo), core: 2. Of those that a mesh axis runs over, the one named last changes fastest.
Arguments:
- visual_encoder_outputs: float32 [131072, 1152], P(('blk', 'group'))
- caption_encoder_outputs: float32 [131072, 1152], P(('blk', 'group'))
- partner_lookup_grid: int32 [2, 64], replicated, may hold values from 0 to 63, as said below
- sharpness_coefficient: float32 [1], replicated, may hold values from 8 to 30
- sigmoid_shift_term: float32 [1], replicated, may hold values from -6 to -2
Outputs:
- image_gradient: float32 [131072, 1152], P(('blk', 'group'))
- text_gradient: float32 [131072, 1152], P(('blk', 'group'))
Inputs may be any that keep to these rules, and one draw needn't show every extreme that they name: In each of the 2 rounds, partner_lookup_grid pairs index b of blk with index b XOR 2**k, where k is a bit position drawn for that round; the rounds' positions differ, so every matching is mutual and no index meets the same partner twice.
All inputs are finite; a program needn't handle non-finite values.
Results may differ from a plain program's by a relative error of at most 0.0049.
Values may be sent and summed in bfloat16 or wider, within the bound.
A program may use at most 64 MiB of HBM per device.

v0:
```python
import jax
import jax.numpy as jnp
from jax import lax
from jax.sharding import PartitionSpec as P

epsilon = 1e-06


def passed_along(x, axis, by):
    count = lax.axis_size(axis)
    return lax.ppermute(x, axis, [(i, (i + by) % count) for i in range(count)])


def normalize(raw_rows):
    radius = jnp.sqrt(jnp.sum(raw_rows * raw_rows, axis=-1, keepdims=True) + epsilon)
    unit_rows = raw_rows / radius
    return (radius, unit_rows, unit_rows.astype(jnp.bfloat16))


def pair_linkage(left_rows, right_rows, similarity_multiplier, offset_value, matched):
    products = lax.dot_general(
        left_rows, right_rows, (((1,), (1,)), ((), ())), preferred_element_type=jnp.float32
    )
    logits = similarity_multiplier * products + offset_value
    if matched:
        labels = 2.0 * jnp.eye(left_rows.shape[0], dtype=jnp.float32) - 1.0
    else:
        labels = -jnp.ones_like(logits)
    weights = -labels * jax.nn.sigmoid(-labels * logits)
    return (similarity_multiplier * weights).astype(jnp.bfloat16)


def toward_left(coupled, right_rows):
    return jnp.dot(coupled, right_rows, preferred_element_type=jnp.float32)


def toward_right(coupled, left_rows):
    return lax.dot_general(
        coupled, left_rows, (((0,), (0,)), ((), ())), preferred_element_type=jnp.float32
    )


def project(radius, unit_rows, gradient):
    radial = jnp.sum(unit_rows * gradient, axis=-1, keepdims=True)
    return (gradient - unit_rows * radial) / radius


def forward_result(stacked, round_masks):
    peer_count = lax.axis_size("blk")
    kind_count, row_count, feature_count = stacked.shape
    piece_rows = row_count // peer_count
    pieces = stacked.reshape(kind_count, peer_count, piece_rows, feature_count)
    spread = lax.all_to_all(pieces, "blk", split_axis=1, concat_axis=1, tiled=True)
    indices = jnp.arange(peer_count, dtype=jnp.int32)
    picked = jnp.concatenate(
        [
            jnp.take(spread, jnp.bitwise_xor(indices, round_mask), axis=1)
            for round_mask in round_masks
        ],
        axis=0,
    )
    received_result = lax.all_to_all(picked, "blk", split_axis=1, concat_axis=1, tiled=True)
    return received_result.reshape(len(round_masks), kind_count, row_count, feature_count)


def arrive_blocks(stacked, round_masks):
    return forward_result(stacked, round_masks)


def on_device(
    visual_encoder_outputs,
    caption_encoder_outputs,
    partner_lookup_grid,
    sharpness_coefficient,
    sigmoid_shift_term,
):
    similarity_multiplier = sharpness_coefficient[0]
    offset_value = sigmoid_shift_term[0]
    image_radius, image_unit, image_half = normalize(visual_encoder_outputs)
    text_radius, text_unit, text_half = normalize(caption_encoder_outputs)
    round_masks = [partner_lookup_grid[number, 0] for number in range(partner_lookup_grid.shape[0])]
    diagonal = pair_linkage(image_half, text_half, similarity_multiplier, offset_value, True)
    image_sum = toward_left(diagonal, text_half)
    text_sum = toward_right(diagonal, image_half)
    prior_text = passed_along(text_half, "group", 1)
    cycle_coupled = pair_linkage(image_half, prior_text, similarity_multiplier, offset_value, False)
    image_sum = image_sum + toward_left(cycle_coupled, prior_text)
    cycle_partial = toward_right(cycle_coupled, image_half).astype(jnp.bfloat16)
    returned = passed_along(cycle_partial, "group", -1)
    text_sum = text_sum + returned.astype(jnp.float32)
    partner_texts = [
        arrive_blocks(text_half[None], [round_mask])[0, 0] for round_mask in round_masks
    ]
    for number in range(len(round_masks)):
        other_text = partner_texts[number]
        coupled = pair_linkage(image_half, other_text, similarity_multiplier, offset_value, False)
        image_sum = image_sum + toward_left(coupled, other_text)
        partial_sum = toward_right(coupled, image_half).astype(jnp.bfloat16)
        sent_back = arrive_blocks(partial_sum[None], [round_masks[number]])[0, 0]
        text_sum = text_sum + sent_back.astype(jnp.float32)
    return (project(image_radius, image_unit, image_sum), project(text_radius, text_unit, text_sum))


def solution(mesh):
    placed = (P(("blk", "group"), None), P(("blk", "group"), None), P(), P(), P())
    return jax.shard_map(
        on_device,
        mesh=mesh,
        in_specs=placed,
        out_specs=(P(("blk", "group"), None), P(("blk", "group"), None)),
        check_vma=False,
    )
```

profile of v0, /device:TPU:33, one launch (start us, length us, event | category | flops | bytes accessed | tf_op | source)
XLA Modules:
  0.0 341.7 jit_solution(17710661071723551896)
XLA Ops:
  4.3 14.0 %all-to-all-start = ((bf16[1,64,8,1152]{3,2,0,1:T(8,128)(2,1)}), bf16[1,64,8,1152]{3,2,0,1:T(8,128)(2,1)S(1)}, u32[]{:S(2)}, u32[]{:S(2)}) async-start(bf16[1,64,8,1152]{3,2,0,1:T(8,128)(2,1)} %fusion.64), calls=%async_computation | async-start | bytes 2359296 | tf_op jit(solution)/shard_map/all_to_all | solution.py:53
  20.2 32.6 %all-to-all-done = bf16[1,64,8,1152]{3,2,0,1:T(8,128)(2,1)S(1)} async-done(((bf16[1,64,8,1152]{3,2,0,1:T(8,128)(2,1)}), bf16[1,64,8,1152]{3,2,0,1:T(8,128)(2,1)S(1)}, u32[]{:S(2)}, u32[]{:S(2)}) %all-to-all-start) | async-done | bytes 1179680 | tf_op jit(solution)/shard_map/all_to_all | solution.py:53
  56.9 5.4 %all-to-all-start.2 = ((bf16[1,64,8,1152]{3,2,0,1:T(8,128)(2,1)}), bf16[1,64,8,1152]{3,2,0,1:T(8,128)(2,1)}, u32[]{:S(2)}, u32[]{:S(2)}) async-start(bf16[1,64,8,1152]{3,2,0,1:T(8,128)(2,1)} %fusion.36), calls=%async_computation.2 | async-start | bytes 2359296 | tf_op jit(solution)/shard_map/all_to_all | solution.py:62
  67.7 28.9 %all-to-all-done.2 = bf16[1,64,8,1152]{3,2,0,1:T(8,128)(2,1)} async-done(((bf16[1,64,8,1152]{3,2,0,1:T(8,128)(2,1)}), bf16[1,64,8,1152]{3,2,0,1:T(8,128)(2,1)}, u32[]{:S(2)}, u32[]{:S(2)}) %all-to-all-start.2) | async-done | bytes 1179680 | tf_op jit(solution)/shard_map/all_to_all | solution.py:62
  96.6 5.2 %all-to-all-start.1 = ((bf16[1,64,8,1152]{3,2,0,1:T(8,128)(2,1)}), bf16[1,64,8,1152]{3,2,0,1:T(8,128)(2,1)S(1)}, u32[]{:S(2)}, u32[]{:S(2)}) async-start(bf16[1,64,8,1152]{3,2,0,1:T(8,128)(2,1)} %fusion.39), calls=%async_computation.1 | async-start | bytes 2359296 | tf_op jit(solution)/shard_map/all_to_all | solution.py:62
  105.8 2.7 fusion.29
  111.2 24.9 %all-to-all-done.1 = bf16[1,64,8,1152]{3,2,0,1:T(8,128)(2,1)S(1)} async-done(((bf16[1,64,8,1152]{3,2,0,1:T(8,128)(2,1)}), bf16[1,64,8,1152]{3,2,0,1:T(8,128)(2,1)S(1)}, u32[]{:S(2)}, u32[]{:S(2)}) %all-to-all-start.1) | async-done | bytes 1179680 | tf_op jit(solution)/shard_map/all_to_all | solution.py:62
  137.1 5.2 %all-to-all-start.5 = ((bf16[1,64,8,1152]{3,2,0,1:T(8,128)(2,1)}), bf16[1,64,8,1152]{3,2,0,1:T(8,128)(2,1)S(1)}, u32[]{:S(2)}, u32[]{:S(2)}) async-start(bf16[1,64,8,1152]{3,2,0,1:T(8,128)(2,1)} %fusion.1), calls=%async_computation.5 | async-start | bytes 2359296 | tf_op jit(solution)/shard_map/all_to_all | solution.py:53
  142.4 2.7 fusion.30
  147.8 28.8 %all-to-all-done.5 = bf16[1,64,8,1152]{3,2,0,1:T(8,128)(2,1)S(1)} async-done(((bf16[1,64,8,1152]{3,2,0,1:T(8,128)(2,1)}), bf16[1,64,8,1152]{3,2,0,1:T(8,128)(2,1)S(1)}, u32[]{:S(2)}, u32[]{:S(2)}) %all-to-all-start.5) | async-done | bytes 1179680 | tf_op jit(solution)/shard_map/all_to_all | solution.py:53
  177.6 5.2 %all-to-all-start.3 = ((bf16[1,64,8,1152]{3,2,0,1:T(8,128)(2,1)}), bf16[1,64,8,1152]{3,2,0,1:T(8,128)(2,1)S(1)}, u32[]{:S(2)}, u32[]{:S(2)}) async-start(bf16[1,64,8,1152]{3,2,0,1:T(8,128)(2,1)} %fusion), calls=%async_computation.3 | async-start | bytes 2359296 | tf_op jit(solution)/shard_map/all_to_all | solution.py:53
  184.9 3.1 gather_fusion.3
  190.6 64.5 %all-to-all-done.3 = bf16[1,64,8,1152]{3,2,0,1:T(8,128)(2,1)S(1)} async-done(((bf16[1,64,8,1152]{3,2,0,1:T(8,128)(2,1)}), bf16[1,64,8,1152]{3,2,0,1:T(8,128)(2,1)S(1)}, u32[]{:S(2)}, u32[]{:S(2)}) %all-to-all-start.3) | async-done | bytes 1179680 | tf_op jit(solution)/shard_map/all_to_all | solution.py:53
  256.1 5.3 %all-to-all-start.6 = ((bf16[1,64,8,1152]{3,2,0,1:T(8,128)(2,1)}), bf16[1,64,8,1152]{3,2,0,1:T(8,128)(2,1)S(1)}, u32[]{:S(2)}, u32[]{:S(2)}) async-start(bf16[1,64,8,1152]{3,2,0,1:T(8,128)(2,1)} %fusion.32), calls=%async_computation.6 | async-start | bytes 2359296 | tf_op jit(solution)/shard_map/all_to_all | solution.py:62
  261.4 2.7 fusion.28
  264.2 3.7 %fusion.43 = f32[512,1152]{1,0:T(8,128)} fusion(bf16[512,512]{1,0:T(8,128)(2,1)S(1)} %fusion.28, bf16[512,1152]{1,0:T(8,128)(2,1)} %fusion.41), kind=kOutput, calls=%fused_computation.80 | convolution fusion | flops 603979776 | bytes 4063232 | tf_op jit(solution)/shard_map/dot_general | solution.py:34
  272.1 3.0 gather_fusion.2
  277.6 6.1 %all-to-all-done.6 = bf16[1,64,8,1152]{3,2,0,1:T(8,128)(2,1)S(1)} async-done(((bf16[1,64,8,1152]{3,2,0,1:T(8,128)(2,1)}), bf16[1,64,8,1152]{3,2,0,1:T(8,128)(2,1)S(1)}, u32[]{:S(2)}, u32[]{:S(2)}) %all-to-all-start.6) | async-done | bytes 1179680 | tf_op jit(solution)/shard_map/all_to_all | solution.py:62
  283.7 6.9 %all-to-all-start.4 = ((bf16[1,64,8,1152]{3,2,0,1:T(8,128)(2,1)}), bf16[1,64,8,1152]{3,2,0,1:T(8,128)(2,1)}, u32[]{:S(2)}, u32[]{:S(2)}) async-start(bf16[1,64,8,1152]{3,2,0,1:T(8,128)(2,1)} %fusion.33), calls=%async_computation.4 | async-start | bytes 2359296 | tf_op jit(solution)/shard_map/all_to_all | solution.py:62
  290.6 3.1 convolution_add_fusion.2
  299.7 19.3 %collective-permute-done.1 = bf16[512,1152]{1,0:T(8,128)(2,1)} collective-permute-done((bf16[512,1152]{1,0:T(8,128)(2,1)}, bf16[512,1152]{1,0:T(8,128)(2,1)}, u32[]{:S(2)}, u32[]{:S(2)}) %collective-permute-start.1) | collective-permute-done | bytes 1179680 | tf_op jit(solution)/shard_map/ppermute | solution.py:11
  319.0 15.2 %all-to-all-done.4 = bf16[1,64,8,1152]{3,2,0,1:T(8,128)(2,1)} async-done(((bf16[1,64,8,1152]{3,2,0,1:T(8,128)(2,1)}), bf16[1,64,8,1152]{3,2,0,1:T(8,128)(2,1)}, u32[]{:S(2)}, u32[]{:S(2)}) %all-to-all-start.4) | async-done | bytes 1179680 | tf_op jit(solution)/shard_map/all_to_all | solution.py:62
  334.2 3.5 %multiply_reduce_fusion = (f32[512]{0:T(512)S(1)}, f32[512,1152]{1,0:T(8,128)S(1)}) fusion(bf16[1,64,8,1152]{3,2,0,1:T(8,128)(2,1)S(1)} %all-to-all-done.6, bf16[1,64,8,1152]{3,2,0,1:T(8,128)(2,1)} %all-to-all-done.4, bf16[512,1152]{1,0:T(8,128)(2,1)} %collective-permute-done.1, f32[512,1152]{1,0:T(8,128)S(1)} %copy-done, f32[512]{0:T(512)S(1)} %add_sqrt_fusion, ...), kind=kOutput, calls=%fused_computation.15 | convolution fusion | flops 609287680 | bytes 9965568 | tf_op jit(solution)/shard_map/dot_general | solution.py:38
  337.8 3.9 %subtract_divide_fusion = f32[512,1152]{1,0:T(8,128)} fusion(f32[512]{0:T(512)S(1)} %get-tuple-element.7, f32[512]{0:T(512)S(1)} %add_sqrt_fusion, bf16[1,64,8,1152]{3,2,0,1:T(8,128)(2,1)S(1)} %all-to-all-done.6, bf16[1,64,8,1152]{3,2,0,1:T(8,128)(2,1)} %all-to-all-done.4, f32[512,1152]{1,0:T(8,128)S(1)} %get-tuple-element.8, ...), kind=kLoop, calls=%fused_computation.14 | loop fusion | flops 5898240 | bytes 10620928 | tf_op jit(solution)/shard_map/div | solution.py:45
  (70 shorter events, 43.2 us)
Async XLA Ops:
  0.6 2.4 copy-start
  4.3 14.0 %copy-start.17 = (s32[2,64]{1,0:T(2,128)S(1)}, s32[2,64]{1,0:T(2,128)}, u32[]{:S(2)}) copy-start(s32[2,64]{1,0:T(2,128)} %param.9) | copy-start | bytes 1540
  4.3 48.5 %all-to-all-start = ((bf16[1,64,8,1152]{3,2,0,1:T(8,128)(2,1)}), bf16[1,64,8,1152]{3,2,0,1:T(8,128)(2,1)S(1)}, u32[]{:S(2)}, u32[]{:S(2)}) async-start(bf16[1,64,8,1152]{3,2,0,1:T(8,128)(2,1)} %fusion.64), calls=%async_computation | async-start | bytes 2359296 | tf_op jit(solution)/shard_map/all_to_all | solution.py:53
  20.1 34.3 %copy-start.16 = (pred[64]{0:T(512)(128)(4,1)}, pred[64]{0:T(512)(128)(4,1)S(1)}, u32[]{:S(2)}) copy-start(pred[64]{0:T(512)(128)(4,1)S(1)} %compare_and_fusion) | copy-start | bytes 196
  56.9 39.6 %all-to-all-start.2 = ((bf16[1,64,8,1152]{3,2,0,1:T(8,128)(2,1)}), bf16[1,64,8,1152]{3,2,0,1:T(8,128)(2,1)}, u32[]{:S(2)}, u32[]{:S(2)}) async-start(bf16[1,64,8,1152]{3,2,0,1:T(8,128)(2,1)} %fusion.36), calls=%async_computation.2 | async-start | bytes 2359296 | tf_op jit(solution)/shard_map/all_to_all | solution.py:62
  63.5 1.7 copy-start.14
  96.6 39.5 %all-to-all-start.1 = ((bf16[1,64,8,1152]{3,2,0,1:T(8,128)(2,1)}), bf16[1,64,8,1152]{3,2,0,1:T(8,128)(2,1)S(1)}, u32[]{:S(2)}, u32[]{:S(2)}) async-start(bf16[1,64,8,1152]{3,2,0,1:T(8,128)(2,1)} %fusion.39), calls=%async_computation.1 | async-start | bytes 2359296 | tf_op jit(solution)/shard_map/all_to_all | solution.py:62
  103.1 2.4 copy-start.1
  105.8 2.7 copy-start.7
  137.1 39.5 %all-to-all-start.5 = ((bf16[1,64,8,1152]{3,2,0,1:T(8,128)(2,1)}), bf16[1,64,8,1152]{3,2,0,1:T(8,128)(2,1)S(1)}, u32[]{:S(2)}, u32[]{:S(2)}) async-start(bf16[1,64,8,1152]{3,2,0,1:T(8,128)(2,1)} %fusion.1), calls=%async_computation.5 | async-start | bytes 2359296 | tf_op jit(solution)/shard_map/all_to_all | solution.py:53
  142.4 3.6 %copy-start.8 = (bf16[512,1152]{1,0:T(8,128)(2,1)S(1)}, bf16[512,1152]{1,0:T(8,128)(2,1)}, u32[]{:S(2)}) copy-start(bf16[512,1152]{1,0:T(8,128)(2,1)} %copy-done.7) | copy-start | bytes 3538948
  177.6 77.4 %all-to-all-start.3 = ((bf16[1,64,8,1152]{3,2,0,1:T(8,128)(2,1)}), bf16[1,64,8,1152]{3,2,0,1:T(8,128)(2,1)S(1)}, u32[]{:S(2)}, u32[]{:S(2)}) async-start(bf16[1,64,8,1152]{3,2,0,1:T(8,128)(2,1)} %fusion), calls=%async_computation.3 | async-start | bytes 2359296 | tf_op jit(solution)/shard_map/all_to_all | solution.py:53
  184.2 83.8 %collective-permute-start = (bf16[512,1152]{1,0:T(8,128)(2,1)}, bf16[512,1152]{1,0:T(8,128)(2,1)}, u32[]{:S(2)}, u32[]{:S(2)}) collective-permute-start(bf16[512,1152]{1,0:T(8,128)(2,1)} %fusion.41), channel_id=1, source_target_pairs={{0,1},{1,2},{2,3},{3,0},{4,5},{5,6},{6,7},{7,4},{8,9},{9,10},{10,1... | collective-permute-start | bytes 3538952 | tf_op jit(solution)/shard_map/ppermute | solution.py:11
  256.1 27.6 %all-to-all-start.6 = ((bf16[1,64,8,1152]{3,2,0,1:T(8,128)(2,1)}), bf16[1,64,8,1152]{3,2,0,1:T(8,128)(2,1)S(1)}, u32[]{:S(2)}, u32[]{:S(2)}) async-start(bf16[1,64,8,1152]{3,2,0,1:T(8,128)(2,1)} %fusion.32), calls=%async_computation.6 | async-start | bytes 2359296 | tf_op jit(solution)/shard_map/all_to_all | solution.py:62
  264.1 3.8 %copy-start.10 = (bf16[512,512]{1,0:T(8,128)(2,1)}, bf16[512,512]{1,0:T(8,128)(2,1)S(1)}, u32[]{:S(2)}) copy-start(bf16[512,512]{1,0:T(8,128)(2,1)S(1)} %fusion.28) | copy-start | bytes 1572868
  264.1 3.8 %copy-start.9 = (bf16[512,1152]{1,0:T(8,128)(2,1)S(1)}, bf16[512,1152]{1,0:T(8,128)(2,1)}, u32[]{:S(2)}) copy-start(bf16[512,1152]{1,0:T(8,128)(2,1)} %copy-done.7) | copy-start | bytes 3538948
  270.2 1.9 copy-start.13
  272.1 46.9 %collective-permute-start.1 = (bf16[512,1152]{1,0:T(8,128)(2,1)}, bf16[512,1152]{1,0:T(8,128)(2,1)}, u32[]{:S(2)}, u32[]{:S(2)}) collective-permute-start(bf16[512,1152]{1,0:T(8,128)(2,1)} %convolution_convert_fusion.2), channel_id=1, source_target_pairs={{0,3},{1,0},{2,1},{3,2},{4,7},{5,4},{6,5},{7,6},{8,11},{9,8},{10,9... | collective-permute-start | bytes 3538952 | tf_op jit(solution)/shard_map/ppermute | solution.py:11
  272.1 3.0 copy-start.15
  283.7 50.6 %all-to-all-start.4 = ((bf16[1,64,8,1152]{3,2,0,1:T(8,128)(2,1)}), bf16[1,64,8,1152]{3,2,0,1:T(8,128)(2,1)}, u32[]{:S(2)}, u32[]{:S(2)}) async-start(bf16[1,64,8,1152]{3,2,0,1:T(8,128)(2,1)} %fusion.33), calls=%async_computation.4 | async-start | bytes 2359296 | tf_op jit(solution)/shard_map/all_to_all | solution.py:62
  290.6 3.2 copy-start.6
  290.6 3.2 copy-start.12
  293.8 1.7 copy-start.2
  293.8 1.7 copy-start.19
  (5 other events, 4.7 us)
where the time goes:
time: 343 us; the launch traced here: 342 us
  waiting for transfers between devices  220 us (64%)
  starting transfers between devices  48.1 us (14%)
  matrix products  29.8 us (9%)
  other arithmetic  25.1 us (7%)
  local copies, waits for them, and re-layouts  16.1 us (5%)
    all_to_all x3, waiting for transfers between devices, forward_result(): lax.all_to_all(pieces, 'blk', split_axis=1, concat_axis=1, tiled=True)  126 us
    all_to_all x4, waiting for transfers between devices, forward_result(): lax.all_to_all(picked, 'blk', split_axis=1, concat_axis=1, tiled=True)  75 us
    all_to_all x3, starting transfers between devices, forward_result(): lax.all_to_all(pieces, 'blk', split_axis=1, concat_axis=1, tiled=True)  24.5 us
    all_to_all x4, starting transfers between devices, forward_result(): lax.all_to_all(picked, 'blk', split_axis=1, concat_axis=1, tiled=True)  22.9 us
    ppermute x2, waiting for transfers between devices, passed_along(): return lax.ppermute(x, axis, [(i, (i + by) % count) for i in range(count)])  19.3 us
    select_n x6, other arithmetic, forward_result(): jnp.take(spread, jnp.bitwise_xor(indices, round_mask), axis=1)  11.3 us
    dot_general x4, matrix products, pair_linkage(): lax.dot_general(left_rows, right_rows, (((1,), (1,)), ((), ())), preferre...  10.4 us
    dot_general x4, matrix products, toward_left(): return jnp.dot(coupled, right_rows, preferred_element_type=jnp.float32)  10.1 us
  transfers between devices with their start and end apart: 9, of which 8 were waited for; matrix products, arithmetic and copies ran while one was open for 15% of the time, Pallas kernels for 0%

commit v1 on v0

v1 whole, which is shorter than its diff:
```python
import functools

import jax
import jax.numpy as jnp
from jax import lax
from jax.experimental import pallas as pl
from jax.experimental.pallas import tpu as pltpu
from jax.sharding import PartitionSpec as P

MESH = pl.DeviceIdType.MESH
epsilon = 1e-06
CHUNKS = 8


def flipped(bits):
    mask = sum(1 << bit for bit in bits)
    return (mask, 0)


def there(move, blk, group, groups):
    mask, step = move
    return (jnp.bitwise_xor(blk, mask), lax.rem(group + step + groups, groups))


def plan(bits):
    transfers = [((0, 1), 0), ((0, -1), 1)]
    low, high = bits
    for bit in bits:
        if bit == 5:
            transfers += [((32, -1), 2), ((32, 1), 3)]
        elif bit == high and (low, high) in ((1, 2), (3, 4)):
            transfers += [(((1 << low) | (1 << high), 0), 4), (((1 << low) | (1 << high), 0), 5)]
        else:
            transfers += [((1 << bit, 0), 0), ((1 << bit, 0), 1)]
    return transfers


def exchange_kernel(transfers, groups, text_ref, image_ref, landed, send_sem, recv_sem):
    blk, group = lax.axis_index("blk"), lax.axis_index("group")
    barrier = pltpu.get_barrier_semaphore()
    moves = []
    for move, _ in transfers:
        for other in (move, (move[0], -move[1])):
            if other not in moves:
                moves.append(other)
    for move in moves:
        pl.semaphore_signal(
            barrier, inc=1, device_id=there(move, blk, group, groups), device_id_type=MESH
        )
    pl.semaphore_wait(barrier, len(moves))
    rows = text_ref.shape[0] // CHUNKS

    def copy(number, chunk):
        move, source = transfers[number]
        span = pl.ds(chunk * rows, rows)
        block = (text_ref, image_ref)[source] if source < 2 else landed.at[source - 2]
        return pltpu.make_async_remote_copy(
            src_ref=block.at[span],
            dst_ref=landed.at[number, span],
            send_sem=send_sem.at[number, chunk],
            recv_sem=recv_sem.at[number, chunk],
            device_id=there(move, blk, group, groups),
            device_id_type=MESH,
        )

    first = [n for n, (_, source) in enumerate(transfers) if source < 2]
    later = [n for n, (_, source) in enumerate(transfers) if source >= 2]
    passed = [transfers[n][1] - 2 for n in later]
    for chunk in range(CHUNKS):
        for number in first:
            copy(number, chunk).start()
    for chunk in range(CHUNKS):
        for number in later:
            copy(transfers[number][1] - 2, chunk).wait_recv()
            copy(number, chunk).start()
    for chunk in range(CHUNKS):
        for number in range(len(transfers)):
            if number not in passed:
                copy(number, chunk).wait_recv()
            copy(number, chunk).wait_send()


def exchange(bits, collective_id, groups, text_half, image_half):
    transfers = plan(bits)
    count = len(transfers)
    return pl.pallas_call(
        functools.partial(exchange_kernel, transfers, groups),
        out_shape=jax.ShapeDtypeStruct((count,) + text_half.shape, jnp.bfloat16),
        in_specs=[pl.BlockSpec(memory_space=pl.ANY)] * 2,
        out_specs=pl.BlockSpec(memory_space=pl.ANY),
        scratch_shapes=[
            pltpu.SemaphoreType.DMA((count, CHUNKS)),
            pltpu.SemaphoreType.DMA((count, CHUNKS)),
        ],
        compiler_params=pltpu.CompilerParams(collective_id=collective_id, has_side_effects=True),
        name="exchange",
    )(text_half, image_half)


def normalize(raw_rows):
    radius = jnp.sqrt(jnp.sum(raw_rows * raw_rows, axis=-1, keepdims=True) + epsilon)
    unit_rows = raw_rows / radius
    return (radius, unit_rows, unit_rows.astype(jnp.bfloat16))


def pair_linkage(left_rows, right_rows, multiplier, offset, matched):
    products = lax.dot_general(
        left_rows, right_rows, (((1,), (1,)), ((), ())), preferred_element_type=jnp.float32
    )
    logits = multiplier * products + offset
    if matched:
        labels = 2.0 * jnp.eye(left_rows.shape[0], dtype=jnp.float32) - 1.0
    else:
        labels = -jnp.ones_like(logits)
    weights = -labels * jax.nn.sigmoid(-labels * logits)
    return (multiplier * weights).astype(jnp.bfloat16)


def toward_left(coupled, right_rows):
    return jnp.dot(coupled, right_rows, preferred_element_type=jnp.float32)


def toward_right(coupled, left_rows):
    return lax.dot_general(
        coupled, left_rows, (((0,), (0,)), ((), ())), preferred_element_type=jnp.float32
    )


def project(radius, unit_rows, gradient):
    radial = jnp.sum(unit_rows * gradient, axis=-1, keepdims=True)
    return (gradient - unit_rows * radial) / radius


def on_device(images, texts, partner_lookup_grid, sharpness_coefficient, sigmoid_shift_term):
    multiplier, offset = sharpness_coefficient[0], sigmoid_shift_term[0]
    groups = lax.axis_size("group")
    bit_count = lax.axis_size("blk").bit_length() - 1
    image_radius, image_unit, image_half = normalize(images)
    text_radius, text_unit, text_half = normalize(texts)
    masks = partner_lookup_grid[:, 0]
    pairs = [(a, b) for a in range(bit_count) for b in range(a + 1, bit_count)]
    wanted = jnp.bitwise_or(masks[0], masks[1])
    branch = sum(
        jnp.where(wanted == (1 << a) + (1 << b), number, 0) for number, (a, b) in enumerate(pairs)
    )
    landed = lax.switch(
        branch,
        [functools.partial(exchange, pair, number, groups) for number, pair in enumerate(pairs)],
        text_half,
        image_half,
    )
    diagonal = pair_linkage(image_half, text_half, multiplier, offset, True)
    image_sum = toward_left(diagonal, text_half)
    text_sum = toward_right(diagonal, image_half)
    for number in range(0, landed.shape[0], 2):
        other_text, other_image = landed[number], landed[number + 1]
        coupled = pair_linkage(image_half, other_text, multiplier, offset, False)
        image_sum = image_sum + toward_left(coupled, other_text)
        coupled = pair_linkage(other_image, text_half, multiplier, offset, False)
        text_sum = text_sum + toward_right(coupled, other_image)
    return (project(image_radius, image_unit, image_sum), project(text_radius, text_unit, text_sum))


def solution(mesh):
    placed = (P(("blk", "group"), None), P(("blk", "group"), None), P(), P(), P())
    return jax.shard_map(
        on_device,
        mesh=mesh,
        in_specs=placed,
        out_specs=(P(("blk", "group"), None), P(("blk", "group"), None)),
        check_vma=False,
    )
```

time: 343 us -> 182 us (0.53)
  the two profiles are of different devices: /device:TPU:33 before, /device:TPU:4 now
where the time goes in v1:
time: 182 us
  Pallas kernels  125 us (69%)
  matrix products  39.8 us (22%)
  other arithmetic  12.1 us (7%)
  between operations  3.34 us (2%)
    pallas_call x1, Pallas kernels, exchange(): pl.pallas_call(functools.partial(exchange_kernel, transfers, groups), out...  125 us
    dot_general x4, matrix products, toward_right(): lax.dot_general(coupled, left_rows, (((0,), (0,)), ((), ())), preferred_e...  19.8 us
    dot_general x4, matrix products, toward_left(): return jnp.dot(coupled, right_rows, preferred_element_type=jnp.float32)  18.9 us
    div x2, other arithmetic, project(): return (gradient - unit_rows * radial) / radius  7.67 us

profile of v1, /device:TPU:4, one launch (start us, length us, event | category | flops | bytes accessed | tf_op | source)
XLA Modules:
  0.0 182.0 jit_solution(14888171687052383660)
XLA Ops:
  0.6 0.0 copy-start.1
  0.6 1.4 fusion.113
  3.4 0.0 copy-start
  3.4 2.0 %multiply_reduce_fusion.2 = f32[512]{0:T(512)S(1)} fusion(f32[512,1152]{1,0:T(8,128)} %param.21), kind=kLoop, calls=%fused_computation.10 | loop fusion | flops 1179136 | bytes 2361344 | tf_op jit(solution)/shard_map/reduce_sum | solution.py:101
  5.4 0.0 copy-done.1
  5.4 0.2 multiply_reduce_fusion.3
  5.7 0.1 copy-done
  5.7 2.1 %fusion.111 = (bf16[512,1152]{1,0:T(8,128)(2,1)S(1)}, bf16[512,1152]{1,0:T(8,128)(2,1)S(1)}) fusion(f32[512,1152]{1,0:T(8,128)} %param.20, f32[512]{0:T(512)S(1)} %add_sqrt_fusion.1, f32[512,1152]{1,0:T(8,128)S(1)} %copy-done, f32[512]{0:T(512)S(1)} %add_sqrt_fusion), kind=kLoop, calls=%fused_computation.117 | loop fusion | flops 2359296 | bytes 7081984 | tf_op jit(solution)/shard_map/convert_element_type | solution.py:103
  7.9 125.3 %conditional.1 = (bf16[6,512,1152]{2,1,0:T(8,128)(2,1)}) conditional(s32[]{:T(128)} %clamp.3, (bf16[512,1152]{1,0:T(8,128)(2,1)S(1)}, bf16[512,1152]{1,0:T(8,128)(2,1)S(1)}) %tuple.175, (bf16[512,1152]{1,0:T(8,128)(2,1)S(1)}, bf16[512,1152]{1,0:T(8,128)(2,1)S(1)}) %tuple.175, (bf16[512,1152]{1,0:T(8,128)(2,1)S(1)}, ...), branch_computations={%region_2.3_spmd, %region_3.4_spmd, %region_4.5_spmd, %region_5.6_... | conditional | bytes 8 | solution.py:146
  7.9 125.1 %exchange.49 = bf16[6,512,1152]{2,1,0:T(8,128)(2,1)} custom-call(bf16[512,1152]{1,0:T(8,128)(2,1)S(1)} %get-tuple-element.290.text_ref, bf16[512,1152]{1,0:T(8,128)(2,1)S(1)} %get-tuple-element.291.image_ref), custom_call_target="tpu_custom_call" | custom-call | tf_op jit(solution)/shard_map/cond/branch_4_fun/exchange/pallas_call | solution.py:86
  134.5 1.1 fusion.44
  135.6 2.3 %fusion.119 = f32[512,1152]{1,0:T(8,128)} fusion(bf16[512,512]{1,0:T(8,128)(2,1)S(1)} %fusion.44, bf16[512,1152]{1,0:T(8,128)(2,1)S(1)} %get-tuple-element.320), kind=kOutput, calls=%fused_computation.121 | convolution fusion | flops 603979776 | bytes 4063232 | tf_op jit(solution)/shard_map/dot_general | solution.py:124
  137.8 5.6 %convolution_add_fusion.2 = f32[512,1152]{1,0:T(8,128)} fusion(f32[512,1152]{1,0:T(8,128)} %fusion.119, bf16[512,1152]{1,0:T(8,128)(2,1)S(1)} %get-tuple-element.321, bf16[6,512,1152]{2,1,0:T(8,128)(2,1)} %get-tuple-element.322, f32[]{:T(128)} %bitcast.75, f32[]{:T(128)} %bitcast.68), kind=kOutput, calls=%fused_computation.2 | convolution fusion | flops 1210384384 | bytes 8258560 | tf_op jit(solution)/shard_map/dot_general | solution.py:124
  143.4 5.5 %convolution_add_fusion.1 = f32[512,1152]{1,0:T(8,128)} fusion(f32[512,1152]{1,0:T(8,128)} %convolution_add_fusion.2, bf16[512,1152]{1,0:T(8,128)(2,1)S(1)} %get-tuple-element.321, bf16[6,512,1152]{2,1,0:T(8,128)(2,1)} %get-tuple-element.322, f32[]{:T(128)} %bitcast.74, f32[]{:T(128)} %bitcast.66), kind=kOutput, calls=%fused_computation.1 | convolution fusion | flops 1210384384 | bytes 8258560 | tf_op jit(solution)/shard_map/dot_general | solution.py:124
  148.9 6.4 %multiply_reduce_fusion = (f32[512]{0:T(512)S(1)}, f32[512,1152]{1,0:T(8,128)}) fusion(f32[512,1152]{1,0:T(8,128)} %param.21, f32[512]{0:T(512)S(1)} %add_sqrt_fusion, f32[512,1152]{1,0:T(8,128)} %convolution_add_fusion.1, bf16[6,512,1152]{2,1,0:T(8,128)(2,1)} %get-tuple-element.322, bf16[512,1152]{1,0:T(8,128)(2,1)S(1)} %get-tuple-element.321, ...), kind=kOutput, calls=%fused_computation.7 | convolution fusion | flops 1212153344 | bytes 10621952 | tf_op jit(solution)/shard_map/dot_general | solution.py:124
  155.4 4.2 %subtract_divide_fusion = f32[512,1152]{1,0:T(8,128)} fusion(f32[512,1152]{1,0:T(8,128)} %get-tuple-element.319, f32[512]{0:T(512)S(1)} %get-tuple-element.318, f32[512]{0:T(512)S(1)} %add_sqrt_fusion, f32[512,1152]{1,0:T(8,128)} %param.21), kind=kLoop, calls=%fused_computation.6 | loop fusion | flops 2359296 | bytes 7081984 | tf_op jit(solution)/shard_map/div | solution.py:131
  159.6 2.2 %fusion.118 = f32[512,1152]{1,0:T(8,128)} fusion(bf16[512,512]{1,0:T(8,128)(2,1)S(1)} %fusion.44, bf16[512,1152]{1,0:T(8,128)(2,1)S(1)} %get-tuple-element.321), kind=kOutput, calls=%fused_computation.120 | convolution fusion | flops 603979776 | bytes 4063232 | tf_op jit(solution)/shard_map/dot_general | solution.py:120
  161.8 5.5 %convolution_add_fusion.5 = f32[512,1152]{1,0:T(8,128)} fusion(f32[512,1152]{1,0:T(8,128)} %fusion.118, bf16[512,1152]{1,0:T(8,128)(2,1)S(1)} %get-tuple-element.320, bf16[6,512,1152]{2,1,0:T(8,128)(2,1)} %get-tuple-element.322, f32[]{:T(128)} %bitcast.78, f32[]{:T(128)} %bitcast.69), kind=kOutput, calls=%fused_computation.5 | convolution fusion | flops 1210384384 | bytes 8258560 | tf_op jit(solution)/shard_map/dot_general | solution.py:120
  167.3 0.0 copy-start.2
  167.3 5.6 %convolution_add_fusion.4 = f32[512,1152]{1,0:T(8,128)} fusion(f32[512,1152]{1,0:T(8,128)} %convolution_add_fusion.5, bf16[512,1152]{1,0:T(8,128)(2,1)S(1)} %get-tuple-element.320, bf16[6,512,1152]{2,1,0:T(8,128)(2,1)} %get-tuple-element.322, f32[]{:T(128)} %bitcast.77, f32[]{:T(128)} %bitcast.67), kind=kOutput, calls=%fused_computation.4 | convolution fusion | flops 1210384384 | bytes 8258560 | tf_op jit(solution)/shard_map/dot_general | solution.py:120
  172.9 0.0 copy-done.2
  173.0 5.5 %multiply_reduce_fusion.1 = (f32[512]{0:T(512)S(1)}, f32[512,1152]{1,0:T(8,128)}) fusion(f32[512,1152]{1,0:T(8,128)S(1)} %copy-done.2, f32[512]{0:T(512)S(1)} %add_sqrt_fusion.1, f32[512,1152]{1,0:T(8,128)} %convolution_add_fusion.4, bf16[6,512,1152]{2,1,0:T(8,128)(2,1)} %get-tuple-element.322, bf16[512,1152]{1,0:T(8,128)(2,1)S(1)} %get-tuple-element.320, ...), kind=kOutput, calls=%fused_computation.9 | convolution fusion | flops 1212153344 | bytes 10621952 | tf_op jit(solution)/shard_map/dot_general | solution.py:120
  178.5 3.5 %subtract_divide_fusion.1 = f32[512,1152]{1,0:T(8,128)} fusion(f32[512,1152]{1,0:T(8,128)} %get-tuple-element.317, f32[512]{0:T(512)S(1)} %get-tuple-element.316, f32[512]{0:T(512)S(1)} %add_sqrt_fusion.1, f32[512,1152]{1,0:T(8,128)S(1)} %copy-done.2), kind=kLoop, calls=%fused_computation.8 | loop fusion | flops 2359296 | bytes 7081984 | tf_op jit(solution)/shard_map/div | solution.py:131
  (2 shorter events, 0.0 us)
Async XLA Ops:
  0.6 4.8 %copy-start.1 = (f32[512,1152]{1,0:T(8,128)S(1)}, f32[512,1152]{1,0:T(8,128)}, u32[]{:S(2)}) copy-start(f32[512,1152]{1,0:T(8,128)} %param.20) | copy-start | bytes 7077892
  3.4 2.4 %copy-start = (f32[512,1152]{1,0:T(8,128)S(1)}, f32[512,1152]{1,0:T(8,128)}, u32[]{:S(2)}) copy-start(f32[512,1152]{1,0:T(8,128)} %param.21) | copy-start | bytes 7077892
  167.3 5.6 %copy-start.2 = (f32[512,1152]{1,0:T(8,128)S(1)}, f32[512,1152]{1,0:T(8,128)}, u32[]{:S(2)}) copy-start(f32[512,1152]{1,0:T(8,128)} %param.20) | copy-start | bytes 7077892

commit v2 on v1

v2 whole, which is shorter than its diff:
```python
import functools

import jax
import jax.numpy as jnp
from jax import lax
from jax.experimental import pallas as pl
from jax.experimental.pallas import tpu as pltpu
from jax.sharding import PartitionSpec as P

MESH = pl.DeviceIdType.MESH
epsilon = 1e-06
CHUNKS = 8
TILE = 256
STRIP = 384


def plan(bits):
    low, high = bits
    streams = [((0, 1), None)]
    for bit in bits:
        if bit == 5:
            streams.append(((32, -1), 0))
        elif bit == high and (low, high) in ((1, 2), (3, 4)):
            streams.append((((1 << low) | (1 << high), 0), 1))
        else:
            streams.append(((1 << bit, 0), None))
    return streams


def fused_kernel(
    streams,
    lag,
    groups,
    image_hbm,
    text_hbm,
    multiplier_ref,
    offset_ref,
    image_out,
    text_out,
    raw,
    half,
    inverse,
    landed,
    coupled,
    total,
    load_sem,
    send_sem,
    recv_sem,
    store_sem,
):
    blk, group = lax.axis_index("blk"), lax.axis_index("group")
    rows_all, width = image_hbm.shape
    rows = rows_all // CHUNKS
    sources, results = (image_hbm, text_hbm), (image_out, text_out)

    def there(move):
        return (jnp.bitwise_xor(blk, move[0]), lax.rem(group + move[1] + groups, groups))

    def span(chunk, size=rows):
        return pl.ds(pl.multiple_of(chunk * size, size), size)

    def part(number):
        return pl.ds(number * rows, rows)

    barrier = pltpu.get_barrier_semaphore()
    moves = []
    for move, _ in streams:
        for other in (move, (move[0], -move[1])):
            if other not in moves:
                moves.append(other)
    for move in moves:
        pl.semaphore_signal(barrier, inc=1, device_id=there(move), device_id_type=MESH)

    def load(kind, chunk):
        return pltpu.make_async_copy(
            sources[kind].at[span(chunk)], raw.at[kind, span(chunk)], load_sem.at[kind, chunk]
        )

    def store(kind, chunk):
        return pltpu.make_async_copy(
            total.at[kind, span(chunk)], results[kind].at[span(chunk)], store_sem.at[kind, chunk]
        )

    def copy(kind, number, chunk):
        (mask, step), origin = streams[number]
        return pltpu.make_async_remote_copy(
            src_ref=landed.at[kind, chunk, part(0 if origin is None else origin + 1)],
            dst_ref=landed.at[kind, chunk, part(number + 1)],
            send_sem=send_sem.at[kind, number, chunk],
            recv_sem=recv_sem.at[kind, number, chunk],
            device_id=there((mask, step * (2 * kind - 1))),
            device_id_type=MESH,
        )

    direct = [n for n, (_, origin) in enumerate(streams) if origin is None]
    passing = [n for n, (_, origin) in enumerate(streams) if origin is not None]
    passed = [streams[n][1] for n in passing]

    @pl.loop(0, CHUNKS)
    def _(chunk):
        for kind in (1, 0):
            load(kind, chunk).start()

    @pl.loop(0, CHUNKS)
    def _(chunk):
        for kind in (0, 1):
            total[kind, span(chunk), :] = jnp.zeros((rows, width), jnp.float32)

    pl.semaphore_wait(barrier, len(moves))

    @pl.loop(0, CHUNKS)
    def _(chunk):
        for kind in (1, 0):
            load(kind, chunk).wait()
            x = raw[kind, span(chunk), :]
            scale = 1.0 / jnp.sqrt(jnp.sum(x * x, axis=-1, keepdims=True) + epsilon)
            inverse[kind, span(chunk), :] = scale
            rounded = (x * scale).astype(jnp.bfloat16)
            half[kind, span(chunk), :] = rounded
            landed[kind, chunk, part(0), :] = rounded
            for number in direct:
                copy(kind, number, chunk).start()

    multiplier, offset = multiplier_ref[0], offset_ref[0]

    def absorb(kind, chunk):
        other = landed.at[1 - kind, chunk]

        @pl.loop(0, rows_all // TILE)
        def _(tile):
            products = lax.dot_general(
                half[kind, span(tile, TILE), :],
                other[...],
                (((1,), (1,)), ((), ())),
                preferred_element_type=jnp.float32,
            )
            logits = multiplier * products + offset
            mine = lax.broadcasted_iota(jnp.int32, logits.shape, 0) + tile * TILE
            theirs = lax.broadcasted_iota(jnp.int32, logits.shape, 1)
            theirs = jnp.where(theirs < rows, theirs + chunk * rows, -1)
            same = mine == theirs
            logits = jnp.where(same, -logits, logits)
            weight = jnp.where(same, -multiplier, multiplier)
            coupled[span(tile, TILE), :] = (weight / (1.0 + jnp.exp(-logits))).astype(jnp.bfloat16)

        @pl.loop(0, width // STRIP)
        def _(number):
            strip = span(number, STRIP)
            total[kind, :, strip] += jnp.dot(
                coupled[...], other[:, strip], preferred_element_type=jnp.float32
            )

    @pl.loop(0, CHUNKS + lag)
    def _(turn):
        if passing:

            @pl.when(turn < CHUNKS)
            def _():
                for kind in (1, 0):
                    for number in passing:
                        copy(kind, streams[number][1], turn).wait_recv()
                        copy(kind, number, turn).start()

        @pl.when(turn >= lag)
        def _():
            chunk = turn - lag

            @pl.loop(0, 2)
            def _(kind):
                for number in range(len(streams)):
                    if number not in passed:
                        copy(1 - kind, number, chunk).wait_recv()
                absorb(kind, chunk)

    @pl.loop(0, CHUNKS)
    def _(chunk):
        for kind in (0, 1):
            scale = inverse[kind, span(chunk), :]
            unit = raw[kind, span(chunk), :] * scale
            gradient = total[kind, span(chunk), :]
            radial = jnp.sum(unit * gradient, axis=-1, keepdims=True)
            total[kind, span(chunk), :] = (gradient - unit * radial) * scale
            store(kind, chunk).start()

    @pl.loop(0, CHUNKS)
    def _(chunk):
        for kind in (0, 1):
            store(kind, chunk).wait()
            for number in range(len(streams)):
                copy(kind, number, chunk).wait_send()


def fused(bits, collective_id, groups, images, texts, multiplier, offset):
    streams = plan(bits)
    lag = 0
    if any(origin is not None for _, origin in streams):
        lag = CHUNKS if 5 in bits else 2
    rows, width = images.shape
    count = len(streams)
    return pl.pallas_call(
        functools.partial(fused_kernel, streams, lag, groups),
        out_shape=[jax.ShapeDtypeStruct((rows, width), jnp.float32)] * 2,
        in_specs=[pl.BlockSpec(memory_space=pl.ANY)] * 2
        + [pl.BlockSpec(memory_space=pltpu.SMEM)] * 2,
        out_specs=[pl.BlockSpec(memory_space=pl.ANY)] * 2,
        scratch_shapes=[
            pltpu.VMEM((2, rows, width), jnp.float32),
            pltpu.VMEM((2, rows, width), jnp.bfloat16),
            pltpu.VMEM((2, rows, 1), jnp.float32),
            pltpu.VMEM((2, CHUNKS, (count + 1) * rows // CHUNKS, width), jnp.bfloat16),
            pltpu.VMEM((rows, (count + 1) * rows // CHUNKS), jnp.bfloat16),
            pltpu.VMEM((2, rows, width), jnp.float32),
            pltpu.SemaphoreType.DMA((2, CHUNKS)),
            pltpu.SemaphoreType.DMA((2, count, CHUNKS)),
            pltpu.SemaphoreType.DMA((2, count, CHUNKS)),
            pltpu.SemaphoreType.DMA((2, CHUNKS)),
        ],
        compiler_params=pltpu.CompilerParams(
            collective_id=collective_id, has_side_effects=True, vmem_limit_bytes=48 << 20
        ),
        name="fused",
    )(images, texts, multiplier, offset)


def on_device(images, texts, partner_lookup_grid, sharpness_coefficient, sigmoid_shift_term):
    groups = lax.axis_size("group")
    bit_count = lax.axis_size("blk").bit_length() - 1
    masks = partner_lookup_grid[:, 0]
    pairs = [(a, b) for a in range(bit_count) for b in range(a + 1, bit_count)]
    wanted = jnp.bitwise_or(masks[0], masks[1])
    branch = sum(
        jnp.where(wanted == (1 << a) + (1 << b), number, 0) for number, (a, b) in enumerate(pairs)
    )
    image_gradient, text_gradient = lax.switch(
        branch,
        [functools.partial(fused, pair, number, groups) for number, pair in enumerate(pairs)],
        images,
        texts,
        sharpness_coefficient,
        sigmoid_shift_term,
    )
    return (image_gradient, text_gradient)


def solution(mesh):
    placed = (P(("blk", "group"), None), P(("blk", "group"), None), P(), P(), P())
    return jax.shard_map(
        on_device,
        mesh=mesh,
        in_specs=placed,
        out_specs=(P(("blk", "group"), None), P(("blk", "group"), None)),
        check_vma=False,
    )
```

time: 182 us -> 82.5 us (0.45)
  Pallas kernels: 125 us -> 74.5 us
  matrix products: 39.8 us -> 0 us
  other arithmetic: 12.1 us -> 0 us
  local copies, waits for them, and re-layouts: 1.44 us -> 5.19 us
    pallas_call x1, Pallas kernels: 125 us -> 74.5 us  [fused(): pl.pallas_call(functools.partial(fused_kernel, streams, lag, groups), out...]
    dot_general x9 -> x0, matrix products: 39.8 us -> none  [the longest x4 19.8 us: toward_right(): lax.dot_general(coupled, left_rows, (((0,), (0,)), ((), ())), preferred_e...]
    div x2 -> x0, other arithmetic: 7.67 us -> none  [project(): return (gradient - unit_rows * radial) / radius]
    unnamed x6 -> x4, local copies, waits for them, and re-layouts: 0.07 us -> 3.91 us
    reduce_sum x2 -> x0, other arithmetic: 2.27 us -> none  [normalize(): jnp.sum(raw_rows * raw_rows, axis=-1, keepdims=True) + epsilon]
    convert_element_type x1 -> x0, other arithmetic: 2.13 us -> none  [normalize(): return (radius, unit_rows, unit_rows.astype(jnp.bfloat16))]
where the time goes in v2:
time: 82.5 us; the launch traced here: 82 us
  Pallas kernels  74.5 us (90%)
  local copies, waits for them, and re-layouts  5.19 us (6%)
  between operations  2.01 us (2%)
    pallas_call x1, Pallas kernels, fused(): pl.pallas_call(functools.partial(fused_kernel, streams, lag, groups), out...  74.5 us
    unnamed x4, local copies, waits for them, and re-layouts  3.91 us

profile of v2, /device:TPU:4, one launch (start us, length us, event | category | flops | bytes accessed | tf_op | source)
XLA Modules:
  0.0 82.0 jit_solution(15575048507406566325)
XLA Ops:
  0.6 1.3 %fusion = (s32[1,1]{1,0:T(1,128)}, s32[1,1]{1,0:T(1,128)}) fusion(s32[2,64]{1,0:T(2,128)} %param.22), kind=kLoop, calls=%fused_computation | loop fusion | bytes 16 | tf_op jit(solution)/shard_map/slice | solution.py:230
  3.3 74.8 %conditional.1 = ((f32[512,1152]{1,0:T(8,128)S(1)}, f32[512,1152]{1,0:T(8,128)})) conditional(s32[]{:T(128)} %clamp.3, (f32[512,1152]{1,0:T(8,128)}, f32[512,1152]{1,0:T(8,128)}, f32[1]{0:T(128)}, f32[1]{0:T(128)}) %tuple.52, (f32[512,1152]{1,0:T(8,128)}, f32[512,1152]{1,0:T(8,128)}, f32[1]{0:T(128)}, ...), branch_computations={%region_0.1_spmd, %region_1.2_spmd, %region_2.3_spmd, %region_3.4_... | conditional | bytes 8 | solution.py:234
  3.3 74.5 %fused.20 = (f32[512,1152]{1,0:T(8,128)S(1)}, f32[512,1152]{1,0:T(8,128)}) custom-call(f32[512,1152]{1,0:T(8,128)} %get-tuple-element.140.image_hbm, f32[512,1152]{1,0:T(8,128)} %get-tuple-element.141.text_hbm, f32[1]{0:T(128)} %get-tuple-element.142.multiplier_ref, f32[1]{0:T(128)} %get-tuple-element.143.offset_ref), custom_call_target="tpu_custom_call" | custom-call | tf_op jit(solution)/shard_map/cond/branch_5_fun/fused/pallas_call | solution.py:200
  78.1 0.0 copy-start
  78.1 1.4 %copy.69 = f32[512,1152]{1,0:T(8,128)} copy(f32[512,1152]{1,0:T(8,128)S(1)} %get-tuple-element.248) | data formatting | bytes 4718592
  79.5 1.1 %copy-done = f32[512,1152]{1,0:T(8,128)S(1)} copy-done((f32[512,1152]{1,0:T(8,128)S(1)}, f32[512,1152]{1,0:T(8,128)}, u32[]{:S(2)}) %copy-start) | copy-done | bytes 2359320
  80.6 1.4 %copy.70 = f32[512,1152]{1,0:T(8,128)} copy(f32[512,1152]{1,0:T(8,128)S(1)} %copy-done) | data formatting | bytes 4718592
Async XLA Ops:
  78.1 2.5 %copy-start = (f32[512,1152]{1,0:T(8,128)S(1)}, f32[512,1152]{1,0:T(8,128)}, u32[]{:S(2)}) copy-start(f32[512,1152]{1,0:T(8,128)} %get-tuple-element.249) | copy-start | bytes 7077892

commit v3 on v2

v3 whole, which is shorter than its diff:
```python
import functools

import jax
import jax.numpy as jnp
from jax import lax
from jax.experimental import pallas as pl
from jax.experimental.pallas import tpu as pltpu
from jax.sharding import PartitionSpec as P

MESH = pl.DeviceIdType.MESH
epsilon = 1e-06
CHUNKS = 16
MERGE = 1
TILE = 512
STRIP = 384
BLOCK = 64


def plan(bits):
    low, high = bits
    streams = [((0, 1), None)]
    for bit in bits:
        if bit == 5:
            streams.append(((32, -1), 0))
        elif bit == high and (low, high) in ((1, 2), (3, 4)):
            streams.append((((1 << low) | (1 << high), 0), 1))
        else:
            streams.append(((1 << bit, 0), None))
    return streams


def normalize_kernel(grid_ref, image_hbm, text_hbm, half, branch_ref, raw, load_sem):
    pairs = all_pairs(grid_ref.shape[1])
    wanted = jnp.bitwise_or(grid_ref[0, 0], grid_ref[1, 0])
    branch = jnp.int32(0)
    for number, (low, high) in enumerate(pairs):
        branch = jnp.where(wanted == (1 << low) + (1 << high), number, branch)
    branch_ref[0] = branch
    steps = image_hbm.shape[0] // BLOCK

    def load(kind, step):
        place = pl.ds(step * BLOCK, BLOCK)
        source = (image_hbm, text_hbm)[kind]
        return pltpu.make_async_copy(source.at[place], raw.at[kind, place], load_sem.at[kind, step])

    for step in range(steps):
        for kind in (1, 0):
            load(kind, step).start()
    for step in range(steps):
        place = pl.ds(step * BLOCK, BLOCK)
        for kind in (1, 0):
            load(kind, step).wait()
        for kind in (1, 0):
            x = raw[kind, place, :]
            scale = 1.0 / jnp.sqrt(jnp.sum(x * x, axis=-1, keepdims=True) + epsilon)
            half[kind, place, :] = (x * scale).astype(jnp.bfloat16)


def normalize(partner_lookup_grid, images, texts):
    rows, width = images.shape
    return pl.pallas_call(
        normalize_kernel,
        out_shape=[pltpu.VMEM((2, rows, width), jnp.bfloat16), jax.ShapeDtypeStruct((1,), jnp.int32)],
        in_specs=[pl.BlockSpec(memory_space=pltpu.SMEM)] + [pl.BlockSpec(memory_space=pltpu.HBM)] * 2,
        out_specs=[
            pl.BlockSpec(memory_space=pltpu.VMEM),
            pl.BlockSpec(memory_space=pltpu.SMEM),
        ],
        scratch_shapes=[
            pltpu.VMEM((2, rows, width), jnp.float32),
            pltpu.SemaphoreType.DMA((2, rows // BLOCK)),
        ],
        compiler_params=pltpu.CompilerParams(vmem_limit_bytes=56 << 20),
        name="normalize",
    )(partner_lookup_grid, images, texts)


def project_kernel(image_hbm, text_hbm, total, image_out, text_out, raw, load_sem, store_sem):
    steps = image_hbm.shape[0] // BLOCK

    def span(step):
        return pl.ds(pl.multiple_of(step * BLOCK, BLOCK), BLOCK)

    def load(kind, step):
        source = (image_hbm, text_hbm)[kind]
        return pltpu.make_async_copy(
            source.at[span(step)], raw.at[kind, span(step)], load_sem.at[kind, step]
        )

    def store(kind, step):
        result = (image_out, text_out)[kind]
        return pltpu.make_async_copy(
            raw.at[kind, span(step)], result.at[span(step)], store_sem.at[kind, step]
        )

    @pl.loop(0, steps)
    def _(step):
        for kind in (0, 1):
            load(kind, step).start()

    @pl.loop(0, steps)
    def _(step):
        for kind in (0, 1):
            load(kind, step).wait()
        results = []
        for kind in (0, 1):
            x = raw[kind, span(step), :]
            gradient = total[kind, span(step), :]
            scale = 1.0 / jnp.sqrt(jnp.sum(x * x, axis=-1, keepdims=True) + epsilon)
            unit = x * scale
            radial = jnp.sum(unit * gradient, axis=-1, keepdims=True)
            results.append((gradient - unit * radial) * scale)
        for kind in (0, 1):
            raw[kind, span(step), :] = results[kind]
        for kind in (0, 1):
            store(kind, step).start()

    @pl.loop(0, steps)
    def _(step):
        for kind in (0, 1):
            store(kind, step).wait()


def project(images, texts, total):
    rows, width = images.shape
    return pl.pallas_call(
        project_kernel,
        out_shape=[jax.ShapeDtypeStruct((rows, width), jnp.float32)] * 2,
        in_specs=[pl.BlockSpec(memory_space=pl.ANY)] * 2 + [pl.BlockSpec(memory_space=pltpu.VMEM)],
        out_specs=[pl.BlockSpec(memory_space=pl.ANY)] * 2,
        scratch_shapes=[
            pltpu.VMEM((2, rows, width), jnp.float32),
            pltpu.SemaphoreType.DMA((2, rows // BLOCK)),
            pltpu.SemaphoreType.DMA((2, rows // BLOCK)),
        ],
        compiler_params=pltpu.CompilerParams(vmem_limit_bytes=16 << 20),
        name="project",
    )(images, texts, total)


def fused_kernel(
    streams,
    lag,
    window,
    groups,
    half,
    multiplier_ref,
    offset_ref,
    total,
    landed,
    coupled,
    send_sem,
    recv_sem,
):
    blk, group = lax.axis_index("blk"), lax.axis_index("group")
    _, rows_all, width = half.shape
    rows = rows_all // CHUNKS
    block = rows * (len(streams) + 1)

    def there(move):
        return (jnp.bitwise_xor(blk, move[0]), lax.rem(group + move[1] + groups, groups))

    def span(chunk, size=rows):
        return pl.ds(pl.multiple_of(chunk * size, size), size)

    def part(chunk, number):
        return pl.ds(pl.multiple_of(chunk * block + number * rows, rows), rows)

    barrier = pltpu.get_barrier_semaphore()
    moves = []
    for move, _ in streams:
        for other in (move, (move[0], -move[1])):
            if other not in moves:
                moves.append(other)
    for move in moves:
        pl.semaphore_signal(barrier, inc=1, device_id=there(move), device_id_type=MESH)

    def copy(kind, number, chunk):
        (mask, step), origin = streams[number]
        block = half.at[kind, span(chunk)]
        if origin is not None:
            block = landed.at[kind, part(chunk, origin + 1)]
        return pltpu.make_async_remote_copy(
            src_ref=block,
            dst_ref=landed.at[kind, part(chunk, number + 1)],
            send_sem=send_sem.at[kind, number, chunk],
            recv_sem=recv_sem.at[kind, number, chunk],
            device_id=there((mask, step * (2 * kind - 1))),
            device_id_type=MESH,
        )

    direct = [n for n, (_, origin) in enumerate(streams) if origin is None]
    passing = [n for n, (_, origin) in enumerate(streams) if origin is not None]
    passed = [streams[n][1] for n in passing]

    pl.semaphore_wait(barrier, len(moves))

    @pl.loop(0, window)
    def _(chunk):
        for kind in (1, 0):
            for number in direct:
                copy(kind, number, chunk).start()

    @pl.loop(0, CHUNKS)
    def _(chunk):
        for kind in (0, 1):
            landed[kind, part(chunk, 0), :] = half[kind, span(chunk), :]
            total[kind, span(chunk), :] = jnp.zeros((rows, width), jnp.float32)

    multiplier, offset = multiplier_ref[0], offset_ref[0]

    def absorb(unit):
        place = span(unit, MERGE * block)

        @pl.loop(0, rows_all // TILE)
        def _(tile):
            products = [
                lax.dot_general(
                    half[kind, span(tile, TILE), :],
                    landed[1 - kind, place, :],
                    (((1,), (1,)), ((), ())),
                    preferred_element_type=jnp.float32,
                )
                for kind in (0, 1)
            ]
            mine = lax.broadcasted_iota(jnp.int32, products[0].shape, 0) + tile * TILE
            theirs = lax.broadcasted_iota(jnp.int32, products[0].shape, 1)
            same = None
            for sub in range(MERGE):
                first = sub * block
                own = (theirs >= first) & (theirs < first + rows)
                own &= mine == theirs + ((unit * MERGE + sub) * rows - first)
                same = own if same is None else same | own
            weight = jnp.where(same, -multiplier, multiplier)
            for kind in (0, 1):
                logits = multiplier * products[kind] + offset
                logits = jnp.where(same, -logits, logits)
                coupled[kind, span(tile, TILE), :] = (weight / (1.0 + jnp.exp(-logits))).astype(
                    jnp.bfloat16
                )

        @pl.loop(0, width // STRIP)
        def _(number):
            strip = span(number, STRIP)
            for kind in (0, 1):
                total[kind, :, strip] += jnp.dot(
                    coupled[kind], landed[1 - kind, place, strip], preferred_element_type=jnp.float32
                )

    @pl.loop(0, CHUNKS + lag)
    def _(turn):
        if passing:

            @pl.when(turn < CHUNKS)
            def _():
                for kind in (1, 0):
                    for number in passing:
                        copy(kind, streams[number][1], turn).wait_recv()
                        copy(kind, number, turn).start()

        if window < CHUNKS:

            @pl.when(turn < CHUNKS - window)
            def _():
                for kind in (1, 0):
                    for number in direct:
                        copy(kind, number, turn + window).start()

        @pl.when((turn >= lag) & (lax.rem(turn - lag, MERGE) == MERGE - 1))
        def _():
            unit = lax.div(turn - lag, MERGE)
            for kind in (1, 0):
                for sub in range(MERGE):
                    for number in range(len(streams)):
                        if number not in passed:
                            copy(kind, number, unit * MERGE + sub).wait_recv()
            absorb(unit)

    @pl.loop(0, CHUNKS)
    def _(chunk):
        for kind in (0, 1):
            for number in range(len(streams)):
                copy(kind, number, chunk).wait_send()


def fused(bits, collective_id, groups, half, images, texts, multiplier, offset):
    streams = plan(bits)
    lag, window = 0, CHUNKS
    if any(origin is not None for _, origin in streams):
        lag, window = (4, 4) if 5 in bits else (2, CHUNKS)
    _, rows, width = half.shape
    count = len(streams)
    total = pl.pallas_call(
        functools.partial(fused_kernel, streams, lag, window, groups),
        out_shape=pltpu.VMEM((2, rows, width), jnp.float32),
        in_specs=[pl.BlockSpec(memory_space=pltpu.VMEM)]
        + [pl.BlockSpec(memory_space=pltpu.SMEM)] * 2,
        out_specs=pl.BlockSpec(memory_space=pltpu.VMEM),
        scratch_shapes=[
            pltpu.VMEM((2, (count + 1) * rows, width), jnp.bfloat16),
            pltpu.VMEM((2, rows, MERGE * (count + 1) * rows // CHUNKS), jnp.bfloat16),
            pltpu.SemaphoreType.DMA((2, count, CHUNKS)),
            pltpu.SemaphoreType.DMA((2, count, CHUNKS)),
        ],
        compiler_params=pltpu.CompilerParams(
            collective_id=collective_id, has_side_effects=True, vmem_limit_bytes=32 << 20
        ),
        name="fused",
    )(half, multiplier, offset)
    return project(images, texts, total)


def all_pairs(peers):
    bit_count = peers.bit_length() - 1
    return [(a, b) for a in range(bit_count) for b in range(a + 1, bit_count)]


def on_device(images, texts, partner_lookup_grid, sharpness_coefficient, sigmoid_shift_term):
    groups = lax.axis_size("group")
    half, branch = normalize(partner_lookup_grid, images, texts)
    image_gradient, text_gradient = lax.switch(
        branch[0],
        [
            functools.partial(fused, pair, number, groups)
            for number, pair in enumerate(all_pairs(lax.axis_size("blk")))
        ],
        half,
        images,
        texts,
        sharpness_coefficient,
        sigmoid_shift_term,
    )
    return (image_gradient, text_gradient)


def solution(mesh):
    placed = (P(("blk", "group"), None), P(("blk", "group"), None), P(), P(), P())
    return jax.shard_map(
        on_device,
        mesh=mesh,
        in_specs=placed,
        out_specs=(P(("blk", "group"), None), P(("blk", "group"), None)),
        check_vma=False,
    )
```

time: 82.5 us -> 78.4 us (0.950)
  local copies, waits for them, and re-layouts: 5.19 us -> 0.01 us
  Pallas kernels: 74.5 us -> 76.1 us
    unnamed x4, local copies, waits for them, and re-layouts: 3.91 us -> 0.01 us
    pallas_call x1 -> x3, Pallas kernels: 74.5 us -> 76.1 us  [the longest x1 67.7 us: fused(): pl.pallas_call(functools.partial(fused_kernel, streams, lag, window, grou...]
    slice x1 -> x0, local copies, waits for them, and re-layouts: 1.27 us -> none  [on_device(): wanted = jnp.bitwise_or(masks[0], masks[1])]
where the time goes in v3:
time: 78.4 us; the launch traced here: 78.3 us
  Pallas kernels  76.1 us (97%)
  between operations  1.54 us (2%)
    pallas_call x1, Pallas kernels, fused(): pl.pallas_call(functools.partial(fused_kernel, streams, lag, window, grou...  67.7 us
    pallas_call x1, Pallas kernels, project(): pl.pallas_call(project_kernel, out_shape=[jax.ShapeDtypeStruct((rows, wid...  4.25 us
    pallas_call x1, Pallas kernels, normalize(): pl.pallas_call(normalize_kernel, out_shape=[pltpu.VMEM((2, rows, width),...  4.18 us

profile of v3, /device:TPU:4, one launch (start us, length us, event | category | flops | bytes accessed | tf_op | source)
XLA Modules:
  0.0 78.3 jit_solution(16857448968115426184)
XLA Ops:
  0.6 0.0 copy-start.1
  0.6 0.0 copy-start
  0.6 4.2 %normalize.1 = (bf16[2,512,1152]{2,1,0:T(8,128)(2,1)S(1)}, s32[1]{0:T(128)}) custom-call(s32[2,64]{1,0:T(2,128)} %grid_ref.1, f32[512,1152]{1,0:T(8,128)} %image_hbm.1, f32[512,1152]{1,0:T(8,128)} %text_hbm.1), custom_call_target="tpu_custom_call" | custom-call | tf_op jit(solution)/shard_map/normalize/pallas_call | solution.py:61
  5.5 0.0 copy-done.1
  5.5 0.0 copy-done
  5.5 72.6 %conditional.1 = ((f32[512,1152]{1,0:T(8,128)}, f32[512,1152]{1,0:T(8,128)})) conditional(s32[]{:T(128)} %bitcast, (bf16[2,512,1152]{2,1,0:T(8,128)(2,1)S(1)}, f32[1]{0:T(128)}, f32[1]{0:T(128)}, f32[512,1152]{1,0:T(8,128)S(1)}, f32[512,1152]{1,0:T(8,128)S(1)}) %tuple.128, (bf16[2,512,1152]{2,1,0:T(8,128)(2,1)S(1)}, ...), branch_computations={%region_0.0_spmd, %region_1.0_spmd, %region_2.0_spmd, %region_3.0_... | conditional | bytes 8 | solution.py:321
  5.8 67.7 %fused.27.total = f32[2,512,1152]{2,1,0:T(8,128)S(1)} custom-call(bf16[2,512,1152]{2,1,0:T(8,128)(2,1)S(1)} %get-tuple-element.212.half, f32[1]{0:T(128)} %get-tuple-element.305.multiplier_ref, f32[1]{0:T(128)} %get-tuple-element.320.offset_ref), custom_call_target="tpu_custom_call" | custom-call | tf_op jit(solution)/shard_map/cond/branch_12_fun/fused/pallas_call | solution.py:293
  73.5 4.3 %project.27 = (f32[512,1152]{1,0:T(8,128)}, f32[512,1152]{1,0:T(8,128)}) custom-call(f32[512,1152]{1,0:T(8,128)S(1)} %get-tuple-element.210.image_hbm, f32[512,1152]{1,0:T(8,128)S(1)} %get-tuple-element.211.text_hbm, f32[2,512,1152]{2,1,0:T(8,128)S(1)} %fused.27.total), custom_call_target="tpu_custom_call" | custom-call | tf_op jit(solution)/shard_map/cond/branch_12_fun/project/pallas_call | solution.py:126
Async XLA Ops:
  0.6 4.9 %copy-start.1 = (f32[512,1152]{1,0:T(8,128)S(1)}, f32[512,1152]{1,0:T(8,128)}, u32[]{:S(2)}) copy-start(f32[512,1152]{1,0:T(8,128)} %text_hbm.1) | copy-start | bytes 7077892
  0.6 4.9 %copy-start = (f32[512,1152]{1,0:T(8,128)S(1)}, f32[512,1152]{1,0:T(8,128)}, u32[]{:S(2)}) copy-start(f32[512,1152]{1,0:T(8,128)} %image_hbm.1) | copy-start | bytes 7077892

commit v4 on v3

--- a/solution.py
+++ b/solution.py
@@ -29,113 +29,67 @@
     return streams
 
 
-def normalize_kernel(grid_ref, image_hbm, text_hbm, half, branch_ref, raw, load_sem):
-    pairs = all_pairs(grid_ref.shape[1])
+def branch_kernel(grid_ref, branch_ref):
     wanted = jnp.bitwise_or(grid_ref[0, 0], grid_ref[1, 0])
     branch = jnp.int32(0)
-    for number, (low, high) in enumerate(pairs):
+    for number, (low, high) in enumerate(all_pairs(grid_ref.shape[1])):
         branch = jnp.where(wanted == (1 << low) + (1 << high), number, branch)
     branch_ref[0] = branch
-    steps = image_hbm.shape[0] // BLOCK
-
-    def load(kind, step):
-        place = pl.ds(step * BLOCK, BLOCK)
-        source = (image_hbm, text_hbm)[kind]
-        return pltpu.make_async_copy(source.at[place], raw.at[kind, place], load_sem.at[kind, step])
-
-    for step in range(steps):
-        for kind in (1, 0):
-            load(kind, step).start()
-    for step in range(steps):
-        place = pl.ds(step * BLOCK, BLOCK)
-        for kind in (1, 0):
-            load(kind, step).wait()
-        for kind in (1, 0):
-            x = raw[kind, place, :]
-            scale = 1.0 / jnp.sqrt(jnp.sum(x * x, axis=-1, keepdims=True) + epsilon)
-            half[kind, place, :] = (x * scale).astype(jnp.bfloat16)
-
-
-def normalize(partner_lookup_grid, images, texts):
-    rows, width = images.shape
+
+
+def find_branch(partner_lookup_grid):
     return pl.pallas_call(
-        normalize_kernel,
-        out_shape=[pltpu.VMEM((2, rows, width), jnp.bfloat16), jax.ShapeDtypeStruct((1,), jnp.int32)],
-        in_specs=[pl.BlockSpec(memory_space=pltpu.SMEM)] + [pl.BlockSpec(memory_space=pltpu.HBM)] * 2,
-        out_specs=[
-            pl.BlockSpec(memory_space=pltpu.VMEM),
-            pl.BlockSpec(memory_space=pltpu.SMEM),
-        ],
+        branch_kernel,
+        out_shape=jax.ShapeDtypeStruct((1,), jnp.int32),
+        in_specs=[pl.BlockSpec(memory_space=pltpu.SMEM)],
+        out_specs=pl.BlockSpec(memory_space=pltpu.SMEM),
+        name="find_branch",
+    )(partner_lookup_grid)[0]
+
+
+def project_kernel(raw, inverse, total, image_out, text_out, results, store_sem):
+    steps = raw.shape[1] // BLOCK
+
+    def span(step):
+        return pl.ds(pl.multiple_of(step * BLOCK, BLOCK), BLOCK)
+
+    def store(kind, step):
+        return pltpu.make_async_copy(
+            results.at[kind, span(step)],
+            (image_out, text_out)[kind].at[span(step)],
+            store_sem.at[kind, step],
+        )
+
+    @pl.loop(0, steps)
+    def _(step):
+        for kind in (0, 1):
+            x, gradient = raw[kind, span(step), :], total[kind, span(step), :]
+            scale = inverse[kind, span(step), :]
+            radial = scale * (scale * jnp.sum(x * gradient, axis=-1, keepdims=True))
+            results[kind, span(step), :] = (gradient - x * radial) * scale
+        for kind in (0, 1):
+            store(kind, step).start()
+
+    @pl.loop(0, steps)
+    def _(step):
+        for kind in (0, 1):
+            store(kind, step).wait()
+
+
+def project(raw, inverse, total):
+    _, rows, width = raw.shape
+    return pl.pallas_call(
+        project_kernel,
+        out_shape=[jax.ShapeDtypeStruct((rows, width), jnp.float32)] * 2,
+        in_specs=[pl.BlockSpec(memory_space=pltpu.VMEM)] * 3,
+        out_specs=[pl.BlockSpec(memory_space=pl.ANY)] * 2,
         scratch_shapes=[
             pltpu.VMEM((2, rows, width), jnp.float32),
             pltpu.SemaphoreType.DMA((2, rows // BLOCK)),
         ],
-        compiler_params=pltpu.CompilerParams(vmem_limit_bytes=56 << 20),
-        name="normalize",
-    )(partner_lookup_grid, images, texts)
-
-
-def project_kernel(image_hbm, text_hbm, total, image_out, text_out, raw, load_sem, store_sem):
-    steps = image_hbm.shape[0] // BLOCK
-
-    def span(step):
-        return pl.ds(pl.multiple_of(step * BLOCK, BLOCK), BLOCK)
-
-    def load(kind, step):
-        source = (image_hbm, text_hbm)[kind]
-        return pltpu.make_async_copy(
-            source.at[span(step)], raw.at[kind, span(step)], load_sem.at[kind, step]
-        )
-
-    def store(kind, step):
-        result = (image_out, text_out)[kind]
-        return pltpu.make_async_copy(
-            raw.at[kind, span(step)], result.at[span(step)], store_sem.at[kind, step]
-        )
-
-    @pl.loop(0, steps)
-    def _(step):
-        for kind in (0, 1):
-            load(kind, step).start()
-
-    @pl.loop(0, steps)
-    def _(step):
-        for kind in (0, 1):
-            load(kind, step).wait()
-        results = []
-        for kind in (0, 1):
-            x = raw[kind, span(step), :]
-            gradient = total[kind, span(step), :]
-            scale = 1.0 / jnp.sqrt(jnp.sum(x * x, axis=-1, keepdims=True) + epsilon)
-            unit = x * scale
-            radial = jnp.sum(unit * gradient, axis=-1, keepdims=True)
-            results.append((gradient - unit * radial) * scale)
-        for kind in (0, 1):
-            raw[kind, span(step), :] = results[kind]
-        for kind in (0, 1):
-            store(kind, step).start()
-
-    @pl.loop(0, steps)
-    def _(step):
-        for kind in (0, 1):
-            store(kind, step).wait()
-
-
-def project(images, texts, total):
-    rows, width = images.shape
-    return pl.pallas_call(
-        project_kernel,
-        out_shape=[jax.ShapeDtypeStruct((rows, width), jnp.float32)] * 2,
-        in_specs=[pl.BlockSpec(memory_space=pl.ANY)] * 2 + [pl.BlockSpec(memory_space=pltpu.VMEM)],
-        out_specs=[pl.BlockSpec(memory_space=pl.ANY)] * 2,
-        scratch_shapes=[
-            pltpu.VMEM((2, rows, width), jnp.float32),
-            pltpu.SemaphoreType.DMA((2, rows // BLOCK)),
-            pltpu.SemaphoreType.DMA((2, rows // BLOCK)),
-        ],
         compiler_params=pltpu.CompilerParams(vmem_limit_bytes=16 << 20),
         name="project",
-    )(images, texts, total)
+    )(raw, inverse, total)
 
 
 def fused_kernel(
@@ -143,17 +97,22 @@
     lag,
     window,
     groups,
-    half,
+    image_hbm,
+    text_hbm,
     multiplier_ref,
     offset_ref,
     total,
+    raw,
+    inverse,
+    half,
     landed,
     coupled,
+    load_sem,
     send_sem,
     recv_sem,
 ):
     blk, group = lax.axis_index("blk"), lax.axis_index("group")
-    _, rows_all, width = half.shape
+    rows_all, width = image_hbm.shape
     rows = rows_all // CHUNKS
     block = rows * (len(streams) + 1)
 
@@ -165,6 +124,18 @@
 
     def part(chunk, number):
         return pl.ds(pl.multiple_of(chunk * block + number * rows, rows), rows)
+
+    def load(kind, step):
+        return pltpu.make_async_copy(
+            (image_hbm, text_hbm)[kind].at[span(step, BLOCK)],
+            raw.at[kind, span(step, BLOCK)],
+            load_sem.at[kind, step],
+        )
+
+    @pl.loop(0, rows_all // BLOCK)
+    def _(step):
+        for kind in (1, 0):
+            load(kind, step).start()
 
     barrier = pltpu.get_barrier_semaphore()
     moves = []
@@ -195,16 +166,32 @@
 
     pl.semaphore_wait(barrier, len(moves))
 
-    @pl.loop(0, window)
-    def _(chunk):
+    @pl.loop(0, rows_all // BLOCK)
+    def _(step):
+        place, count = span(step, BLOCK), BLOCK // rows
         for kind in (1, 0):
-            for number in direct:
-                copy(kind, number, chunk).start()
+            load(kind, step).wait()
+        for kind in (1, 0):
+            x = raw[kind, place, :]
+            scale = 1.0 / jnp.sqrt(jnp.sum(x * x, axis=-1, keepdims=True) + epsilon)
+            inverse[kind, place, :] = scale
+            rounded = (x * scale).astype(jnp.bfloat16)
+            half[kind, place, :] = rounded
+            for sub in range(count):
+                own = part(step * count + sub, 0)
+                landed[kind, own, :] = rounded[sub * rows : (sub + 1) * rows]
+        for sub in range(count):
+            chunk = step * count + sub
+
+            @pl.when(chunk < window)
+            def _():
+                for kind in (1, 0):
+                    for number in direct:
+                        copy(kind, number, chunk).start()
 
     @pl.loop(0, CHUNKS)
     def _(chunk):
         for kind in (0, 1):
-            landed[kind, part(chunk, 0), :] = half[kind, span(chunk), :]
             total[kind, span(chunk), :] = jnp.zeros((rows, width), jnp.float32)
 
     multiplier, offset = multiplier_ref[0], offset_ref[0]
@@ -283,31 +270,37 @@
                 copy(kind, number, chunk).wait_send()
 
 
-def fused(bits, collective_id, groups, half, images, texts, multiplier, offset):
+def fused(bits, collective_id, groups, images, texts, multiplier, offset):
     streams = plan(bits)
     lag, window = 0, CHUNKS
     if any(origin is not None for _, origin in streams):
         lag, window = (4, 4) if 5 in bits else (2, CHUNKS)
-    _, rows, width = half.shape
+    rows, width = images.shape
     count = len(streams)
-    total = pl.pallas_call(
+    total, raw, inverse = pl.pallas_call(
         functools.partial(fused_kernel, streams, lag, window, groups),
-        out_shape=pltpu.VMEM((2, rows, width), jnp.float32),
-        in_specs=[pl.BlockSpec(memory_space=pltpu.VMEM)]
+        out_shape=[
+            pltpu.VMEM((2, rows, width), jnp.float32),
+            pltpu.VMEM((2, rows, width), jnp.float32),
+            pltpu.VMEM((2, rows, 1), jnp.float32),
+        ],
+        in_specs=[pl.BlockSpec(memory_space=pl.ANY)] * 2
         + [pl.BlockSpec(memory_space=pltpu.SMEM)] * 2,
-        out_specs=pl.BlockSpec(memory_space=pltpu.VMEM),
+        out_specs=[pl.BlockSpec(memory_space=pltpu.VMEM)] * 3,
         scratch_shapes=[
+            pltpu.VMEM((2, rows, width), jnp.bfloat16),
             pltpu.VMEM((2, (count + 1) * rows, width), jnp.bfloat16),
             pltpu.VMEM((2, rows, MERGE * (count + 1) * rows // CHUNKS), jnp.bfloat16),
+            pltpu.SemaphoreType.DMA((2, rows // BLOCK)),
             pltpu.SemaphoreType.DMA((2, count, CHUNKS)),
             pltpu.SemaphoreType.DMA((2, count, CHUNKS)),
         ],
         compiler_params=pltpu.CompilerParams(
-            collective_id=collective_id, has_side_effects=True, vmem_limit_bytes=32 << 20
+            collective_id=collective_id, has_side_effects=True, vmem_limit_bytes=50 << 20
         ),
         name="fused",
-    )(half, multiplier, offset)
-    return project(images, texts, total)
+    )(images, texts, multiplier, offset)
+    return project(raw, inverse, total)
 
 
 def all_pairs(peers):
@@ -317,14 +310,13 @@
 
 def on_device(images, texts, partner_lookup_grid, sharpness_coefficient, sigmoid_shift_term):
     groups = lax.axis_size("group")
-    half, branch = normalize(partner_lookup_grid, images, texts)
+    branch = find_branch(partner_lookup_grid)
     image_gradient, text_gradient = lax.switch(
-        branch[0],
+        branch,
         [
             functools.partial(fused, pair, number, groups)
             for number, pair in enumerate(all_pairs(lax.axis_size("blk")))
         ],
-        half,
         images,
         texts,
         sharpness_coefficient,

time: 78.4 us -> 69.9 us (0.89)
  Pallas kernels: 76.1 us -> 66.8 us
    pallas_call x1, Pallas kernels: 67.7 us -> 62.8 us  [fused(): pl.pallas_call(functools.partial(fused_kernel, streams, lag, window, grou...]
    pallas_call x1, Pallas kernels: 4.18 us -> 1.22 us  [find_branch(): pl.pallas_call(branch_kernel, out_shape=jax.ShapeDtypeStruct((1,), jnp.in...]
    pallas_call x1, Pallas kernels: 4.25 us -> 2.79 us  [project(): pl.pallas_call(project_kernel, out_shape=[jax.ShapeDtypeStruct((rows, wid...]
where the time goes in v4:
time: 69.9 us; the launch traced here: 69.1 us
  Pallas kernels  66.8 us (96%)
  between operations  1.51 us (2%)
  loops' own time  0.77 us (1%)
    pallas_call x1, Pallas kernels, fused(): pl.pallas_call(functools.partial(fused_kernel, streams, lag, window, grou...  62.8 us
    pallas_call x1, Pallas kernels, project(): pl.pallas_call(project_kernel, out_shape=[jax.ShapeDtypeStruct((rows, wid...  2.79 us

profile of v4, /device:TPU:4, one launch (start us, length us, event | category | flops | bytes accessed | tf_op | source)
XLA Modules:
  0.0 69.1 jit_solution(13617562880658877339)
XLA Ops:
  0.6 1.2 %find_branch.1 = s32[1]{0:T(128)} custom-call(s32[2,64]{1,0:T(2,128)} %grid_ref.1), custom_call_target="tpu_custom_call" | custom-call | tf_op jit(solution)/shard_map/find_branch/pallas_call | solution.py:41
  2.5 66.3 %conditional.1 = ((f32[512,1152]{1,0:T(8,128)}, f32[512,1152]{1,0:T(8,128)})) conditional(s32[]{:T(128)} %bitcast, (f32[512,1152]{1,0:T(8,128)}, f32[512,1152]{1,0:T(8,128)}, f32[1]{0:T(128)}, f32[1]{0:T(128)}) %tuple.52, (f32[512,1152]{1,0:T(8,128)}, f32[512,1152]{1,0:T(8,128)}, f32[1]{0:T(128)}, ...), branch_computations={%region_0.0_spmd, %region_1.0_spmd, %region_2.0_spmd, %region_3.0_... | conditional | bytes 8 | solution.py:314
  2.7 62.8 %fused.21 = (f32[2,512,1152]{2,1,0:T(8,128)S(1)}, f32[2,512,1152]{2,1,0:T(8,128)S(1)}, f32[2,512,1]{2,1,0:T(8,128)S(1)}) custom-call(f32[512,1152]{1,0:T(8,128)} %get-tuple-element.162.image_hbm, f32[512,1152]{1,0:T(8,128)} %get-tuple-element.163.text_hbm, f32[1]{0:T(128)} %get-tuple-element.164.multiplier_ref, f32[1]{0:T(128)} %get-tuple-element.165.offset_ref), custom_call_target="tpu_custom_call" | custom-call | tf_op jit(solution)/shard_map/cond/branch_6_fun/fused/pallas_call | solution.py:280
  65.5 2.8 %project.21 = (f32[512,1152]{1,0:T(8,128)}, f32[512,1152]{1,0:T(8,128)}) custom-call(f32[2,512,1152]{2,1,0:T(8,128)S(1)} %get-tuple-element.166.raw, f32[2,512,1]{2,1,0:T(8,128)S(1)} %get-tuple-element.167.inverse, f32[2,512,1152]{2,1,0:T(8,128)S(1)} %get-tuple-element.168.total), custom_call_target="tpu_custom_call" | custom-call | tf_op jit(solution)/shard_map/cond/branch_6_fun/project/pallas_call | solution.py:81
